TPU v7x, 1024 devices: a whole 4x8x16 slice. The times are simulated.
1024 devices in a mesh: dp: 4 (over y_hi), row: 8 (over x, core), col: 32 (over y_lo, z).
Axes of the slice: x: 4, y: 8 (y_hi: 4, y_lo: 2; y = y_hi * 2 + y_lo), z: 16, core: 2. Of those that a mesh axis runs over, the one named last changes fastest.
Arguments:
- grad_out: bfloat16 [1024, 8192], P(('dp', 'col'), 'row'), may hold values from -6 to 6
- saved_hidden: bfloat16 [1024, 26624], P(('dp', 'row'), 'col'), may hold values from -0.1875 to 0.1875
- down_weight: bfloat16 [26624, 8192], P('col', 'row'), may hold values from -0.0625 to 0.0625
Outputs:
- input_grad: bfloat16 [1024, 26624], P(('dp', 'row'), 'col')
- weight_grad: bfloat16 [26624, 8192], P(('col', 'dp'), 'row')
All inputs are finite; a program needn't handle non-finite values.
Results may differ from a plain program's by a relative error of at most 0.001.
Values may be sent and summed in bfloat16 or wider, within the bound.
A program may use at most 32 MiB of HBM per device.

v0:
```python
import jax
import jax.numpy as jnp
from jax import lax
from jax.sharding import PartitionSpec as P


def local(grad_out, saved_hidden, down_weight):
    grad_copy = lax.all_gather(grad_out, "col", axis=0, tiled=True)
    hidden_copy = lax.all_gather(saved_hidden, "row", axis=0, tiled=True)
    partial_grad = lax.dot_general(
        hidden_copy, grad_copy, (((0,), (0,)), ((), ())), preferred_element_type=jnp.float32
    )
    weight_grad = lax.psum_scatter(partial_grad, "dp", scatter_dimension=0, tiled=True)
    input_grad = lax.psum_scatter(
        lax.dot_general(
            grad_copy, down_weight, (((1,), (1,)), ((), ())), preferred_element_type=jnp.float32
        ),
        "row",
        scatter_dimension=0,
        tiled=True,
    )
    return (input_grad.astype(jnp.bfloat16), weight_grad.astype(jnp.bfloat16))


def solution(mesh):
    placed = (P(("dp", "col"), "row"), P(("dp", "row"), "col"), P("col", "row"))
    return jax.shard_map(
        local,
        mesh=mesh,
        in_specs=placed,
        out_specs=(P(("dp", "row"), "col"), P(("col", "dp"), "row")),
        check_vma=False,
    )
```

profile of v0, /device:TPU:5, one launch (start us, length us, event | category | flops | bytes accessed | tf_op | source)
XLA Modules:
  0.0 211.7 jit_solution(10963384222536965693)
XLA Ops:
  7.2 0.0 copy-start
  7.2 0.0 reduce-scatter.3.cloned.1.call-start
  7.2 65.3 %all_gather.6 = bf16[256,1024]{1,0:T(8,128)(2,1)S(1)} all-gather(bf16[8,1024]{1,0:T(8,128)(2,1)} %param.3), channel_id=1, replica_groups=mesh['dp'=4,'row'=8,'col'=32] {'col'}, dimensions={0}, use_global_device_ids=true | all-gather | bytes 540672 | tf_op jit(solution)/shard_map/all_gather | solution.py:8
  72.5 0.0 copy-done
  72.5 0.0 copy-start.1
  72.5 1.7 fusion
  74.2 0.0 reduce-scatter.3.cloned.1.call-update
  74.3 0.0 reduce-scatter.5.cloned.1.call-start
  74.3 0.0 copy-done.1
  74.3 26.0 %all_gather.7 = bf16[256,832]{1,0:T(8,128)(2,1)S(1)} all-gather(bf16[32,832]{1,0:T(8,128)(2,1)S(1)} %copy-done.1), channel_id=1, replica_groups=mesh['dp'=4,'row'=8,'col'=32] {'row'}, dimensions={0}, use_global_device_ids=true | all-gather | bytes 479232 | tf_op jit(solution)/shard_map/all_gather | solution.py:9
  100.3 2.4 %fusion.1 = f32[832,1024]{1,0:T(8,128)} fusion(bf16[256,832]{1,0:T(8,128)(2,1)S(1)} %all_gather.7, bf16[256,1024]{1,0:T(8,128)(2,1)S(1)} %all_gather.6), kind=kOutput, calls=%fused_computation.1 | convolution fusion | flops 436207616 | bytes 4358144 | tf_op jit(solution)/shard_map/dot_general | solution.py:10
  102.7 0.0 reduce-scatter.5.cloned.1.call-update
  102.7 15.8 %reduce-scatter.3.cloned.1.call-done = f32[32,832]{1,0:T(8,128)} async-done(((f32[256,832]{1,0:T(8,128)}), f32[32,832]{1,0:T(8,128)}) %reduce-scatter.3.cloned.1.call-update) | async-done | bytes 106512 | tf_op jit(solution)/shard_map/reduce_scatter | solution.py:14
  118.5 1.5 convert_element_type.6
  120.0 82.8 %reduce-scatter.5.cloned.1.call-done = f32[208,1024]{1,0:T(8,128)} async-done(((f32[832,1024]{1,0:T(8,128)}), f32[208,1024]{1,0:T(8,128)}) %reduce-scatter.5.cloned.1.call-update) | async-done | bytes 851984 | tf_op jit(solution)/shard_map/reduce_scatter | solution.py:13
  202.9 2.0 convert_element_type.7
Async XLA Ops:
  7.2 65.4 %copy-start = (bf16[832,1024]{1,0:T(8,128)(2,1)S(1)}, bf16[832,1024]{1,0:T(8,128)(2,1)}, u32[]{:S(2)}) copy-start(bf16[832,1024]{1,0:T(8,128)(2,1)} %param.5) | copy-start | bytes 5111812
  7.2 111.3 %reduce-scatter.3.cloned.1.call-start = ((), (), s32[]{:S(2)}) async-start(), calls=%async_computation.2 | async-start | bytes 1032192 | tf_op jit(solution)/shard_map/reduce_scatter | solution.py:14
  72.5 1.8 copy-start.1
  74.3 128.6 %reduce-scatter.5.cloned.1.call-start = ((), (), s32[]{:S(2)}) async-start(), calls=%async_computation.3 | async-start | bytes 4259840 | tf_op jit(solution)/shard_map/reduce_scatter | solution.py:13
Sparse Core Ops, SparseCore 0:
  74.4 44.0 reduce-scatter.2
  122.3 80.4 reduce-scatter.4
where the time goes:
time: 212 us
  waiting for transfers between devices  98.7 us (47%)
  blocking collectives  91.3 us (43%)
  between operations  14.1 us (7%)
  matrix products  4.05 us (2%)
  other arithmetic  3.5 us (2%)
    reduce_scatter x1, waiting for transfers between devices, local(): lax.psum_scatter(partial_grad, 'dp', scatter_dimension=0, tiled=True)  82.8 us
    all_gather x1, blocking collectives, local(): grad_copy = lax.all_gather(grad_out, 'col', axis=0, tiled=True)  65.3 us
    all_gather x1, blocking collectives, local(): hidden_copy = lax.all_gather(saved_hidden, 'row', axis=0, tiled=True)  26 us
    reduce_scatter x1, waiting for transfers between devices, local(): lax.psum_scatter(lax.dot_general(grad_copy, down_weight, (((1,), (1,)), (...  15.8 us
  transfers between devices with their start and end apart: 2, of which 2 were waited for; matrix products, arithmetic and copies ran while one was open for 2% of the time, Pallas kernels for 0%

commit v1 on v0

v1 whole, which is shorter than its diff:
```python
import functools

import jax
import jax.numpy as jnp
from jax import lax
from jax.experimental import pallas as pl
from jax.experimental.pallas import tpu as pltpu
from jax.sharding import PartitionSpec as P

MESH = pl.DeviceIdType.MESH
F32, BF16 = jnp.float32, jnp.bfloat16
LAG = 1


def rel_of(slot, n):
    return (-(slot + 1) // 2 if slot % 2 else slot // 2) % n


def groups_of(n):
    return [(0, 1)] + [(2 * g - 1, 2) for g in range(1, n // 2)] + [(n - 1, 1)]


def kernel(nx, ny, nz, g_hbm, h_hbm, w_hbm, ig_ref, wg_ref, gb, hv, hs, hb, ht, wv, ps, pr, rr, acc,
           lsem, zs, zr, ys, yr, hss, hrs, iss, irs):
    ndp = ny // 2
    hid = h_hbm.shape[1]
    quarter = hid // ndp
    tg, cols = g_hbm.shape
    th = h_hbm.shape[0]
    dp, row, col = (lax.axis_index(a) for a in ("dp", "row", "col"))
    y, z = dp * 2 + lax.div(col, nz), lax.rem(col, nz)
    y_lo = lax.div(col, nz)
    x, c = lax.div(row, 2), lax.rem(row, 2)

    def at(x_=None, y_=None, z_=None, c_=None):
        xx = x if x_ is None else lax.rem(x + x_ + nx, nx)
        yy = y if y_ is None else lax.rem(y + y_ + ny, ny)
        zz = z if z_ is None else lax.rem(z + z_ + nz, nz)
        cc = c if c_ is None else 1 - c
        return (lax.div(yy, 2), xx * 2 + cc, lax.rem(yy, 2) * nz + zz)

    load_g = pltpu.make_async_copy(g_hbm, gb.at[0, 0], lsem.at[0])
    load_h = pltpu.make_async_copy(h_hbm, hv, lsem.at[1])
    load_w = pltpu.make_async_copy(w_hbm, wv, lsem.at[2])
    load_g.start()
    load_h.start()
    load_w.start()
    barrier = pltpu.get_barrier_semaphore()
    peers = (
        [at(z_=d) for d in range(1, nz)]
        + [at(y_=d) for d in sorted({1, ny - 1} | set(range(2, ny, 2)))]
        + [at(x_=d) for d in range(1, nx)]
        + [at(c_=1)]
    )
    for p in peers:
        pl.semaphore_signal(barrier, inc=1, device_id=p, device_id_type=MESH)
    load_h.wait()
    hs[...] = jnp.zeros_like(hs)
    for k in range(ndp):
        hs[k, :, :quarter] = hv[:, k * quarter:(k + 1) * quarter]
    load_g.wait()
    pl.semaphore_wait(barrier, len(peers))

    def remote(src, dst, ss, rs, to):
        return pltpu.make_async_remote_copy(src_ref=src, dst_ref=dst, send_sem=ss, recv_sem=rs, device_id=to, device_id_type=MESH)

    sent = []

    zc = {}
    for s in range(1, nz):
        zc[s] = remote(gb.at[0, 0], gb.at[0, s], zs.at[s], zr.at[s], at(z_=-rel_of(s, nz) % nz))
    zgroups = groups_of(nz)
    ng = len(zgroups)
    top = ny // 2

    def y_copy(up, level, g):
        s0, n = zgroups[g]
        if level == top:
            if n == 2:
                s0, n = s0 + (0 if up else 1), 1
            elif (g == 0) != up:
                return None
        frm = 0 if level == 1 else (2 * level - 3 if up else 2 * level - 2)
        to = ny - 1 if level == top else (2 * level - 1 if up else 2 * level)
        k = ((level - 1) * 2 + (0 if up else 1)) * ng + g
        return remote(gb.at[frm, pl.ds(s0, n)], gb.at[to, pl.ds(s0, n)], ys.at[k], yr.at[k], at(y_=1 if up else -1))

    yc = {(u, l, g): y_copy(u, l, g) for u in (True, False) for l in range(1, top + 1) for g in range(ng)}

    def send(cp):
        if cp is not None:
            cp.start()
            sent.append(cp)

    def y_send(level, g):
        for u in (True, False):
            send(yc[u, level, g])

    y_send(1, 0)
    for s in range(1, nz):
        send(zc[s])
    h1 = []
    for j, d in enumerate(range(2, ny, 2)):
        to_dp = lax.rem(dp + d // 2, ndp)
        h1.append(remote(hs.at[to_dp], hb.at[row, dp], hss.at[j], hrs.at[j], at(y_=d)))
        send(h1[-1])
    hb[row, dp] = hs[dp]
    h2 = [remote(hb.at[row], hb.at[row], hss.at[ndp + j], hrs.at[ndp + j], at(x_=d)) for j, d in enumerate(range(1, nx))]
    h3 = []
    for j in range(nx):
        r = lax.rem(x + nx - j, nx) * 2 + c
        k = ndp + nx + j
        h3.append(remote(hb.at[r], hb.at[r], hss.at[k], hrs.at[k], at(c_=1)))

    def do_h2():
        for cp in h1:
            cp.wait_recv()
        for cp in h2:
            send(cp)
        send(h3[0])

    def do_h3():
        for j, cp in enumerate(h2):
            cp.wait_recv()
            send(h3[j + 1])

    def do_ht():
        for cp in h3:
            cp.wait_recv()
        tok = nz * tg
        a = lax.broadcasted_iota(jnp.int32, (tok, tok), 0)
        b = lax.broadcasted_iota(jnp.int32, (tok, tok), 1)
        slot = lax.div(b, tg)
        half = lax.div(slot + 1, 2)
        rel = jnp.where(lax.rem(slot, 2) == 1, nz - half, half)
        want = lax.rem(z + rel, nz) * tg + lax.rem(b, tg)
        perm = jnp.where(a == want, 1.0, 0.0).astype(BF16)
        nr = tok // th
        for o in range(ny):
            yy = lax.rem(y + rel_of(o, ny), ny)
            blk = hb[pl.ds(lax.rem(yy, 2) * nr, nr), lax.div(yy, 2)].reshape(tok, hs.shape[2])
            got = lax.dot_general(blk, perm, (((0,), (0,)), ((), ())), preferred_element_type=F32)
            ht[o] = got.astype(BF16)

    def partial(block, of_y):
        xg = gb[block].reshape(nz * tg, cols)
        p = lax.dot_general(xg, wv[...], (((1,), (1,)), ((), ())), preferred_element_type=F32)
        per = th // tg
        for s in range(nz):
            za = lax.rem(z + rel_of(s, nz), nz)
            r = of_y * (nz // per) + lax.div(za, per)
            ps[lax.rem(r, 2), lax.div(r, 2), lax.rem(za, per)] = p[s * tg:(s + 1) * tg]

    r1 = remote(ps.at[1 - c], pr, iss.at[0], irs.at[0], at(c_=1))
    r2 = []
    for j, d in enumerate(range(1, nx)):
        r2.append(remote(pr.at[lax.rem(x + d, nx)], rr.at[j], iss.at[1 + j], irs.at[1 + j], at(x_=d)))

    def do_own():
        load_w.wait()
        partial(0, y_lo)

    def do_pair():
        partial(jnp.where(y_lo == 0, 2, 1) if top > 1 else 1, 1 - y_lo)
        send(r1)

    def do_r2():
        r1.wait_recv()
        for j, d in enumerate(range(1, nx)):
            k = lax.rem(x + d, nx)
            pr[k] = pr[k] + ps[c, k]
            send(r2[j])

    def do_r3():
        total = pr[x] + ps[c, x]
        for j, cp in enumerate(r2):
            cp.wait_recv()
            total = total + rr[j]
        ig_ref[...] = total.reshape(th, hid).astype(BF16)

    def weight(lo, hi, first):
        t = None
        for o in range(lo, hi):
            d = jnp.dot(ht[o], gb[o].reshape(nz * tg, cols), preferred_element_type=F32)
            t = d if t is None else t + d
        t = t[:quarter]
        return t if first else acc[...] + t

    def z_step(g):
        s0, n = zgroups[g]
        if g:
            for s in range(s0, s0 + n):
                zc[s].wait_recv()
            y_send(1, g)

    def y_step(level, g):
        for u in (True, False):
            if yc[u, level, g] is not None:
                yc[u, level, g].wait_recv()
        if level < top:
            y_send(level + 1, g)

    rounds = ng + LAG * top
    done = set()
    for r in range(rounds + 1):
        if r < ng:
            z_step(r)
        for level in range(1, top):
            g = r - LAG * level
            if 0 <= g < ng:
                y_step(level, g)
        if r == 2:
            do_h2()
        if r == 4:
            do_h3()
        if r == 5:
            do_ht()
        if r == ng - 1:
            do_own()
        if r == ng - 1 + LAG:
            do_pair()
        if r == ng + 2 * LAG:
            do_r2()
    cut = 2 * min(2, top - 1) + 1
    acc[...] = weight(0, cut, True)
    do_r3()
    for g in range(ng):
        y_step(top, g)
    wg_ref[...] = weight(cut, ny, False).astype(BF16)
    for cp in sent:
        cp.wait_send()


def local(nx, ny, nz, grad_out, saved_hidden, down_weight):
    tg, cols = grad_out.shape
    th, hid = saved_hidden.shape
    ndp = ny // 2
    quarter = hid // ndp
    wide = -(-quarter // 128) * 128
    top = ny // 2
    nyc = 2 * top * (nz // 2 + 1)
    dma = pltpu.SemaphoreType.DMA
    return pl.pallas_call(
        functools.partial(kernel, nx, ny, nz),
        out_shape=(jax.ShapeDtypeStruct((th, hid), BF16), jax.ShapeDtypeStruct((quarter, cols), BF16)),
        in_specs=[pl.BlockSpec(memory_space=pl.ANY)] * 3,
        out_specs=(pl.BlockSpec(memory_space=pltpu.VMEM),) * 2,
        scratch_shapes=[
            pltpu.VMEM((ny, nz, tg, cols), BF16),
            pltpu.VMEM((th, hid), BF16),
            pltpu.VMEM((ndp, th, wide), BF16),
            pltpu.VMEM((2 * nx, ndp, th, wide), BF16),
            pltpu.VMEM((ny, wide, nz * tg), BF16),
            pltpu.VMEM(down_weight.shape, BF16),
            pltpu.VMEM((2, nx, th // tg, tg, hid), F32),
            pltpu.VMEM((nx, th // tg, tg, hid), F32),
            pltpu.VMEM((nx - 1, th // tg, tg, hid), F32),
            pltpu.VMEM((quarter, cols), F32),
            dma((3,)), dma((nz,)), dma((nz,)), dma((nyc,)), dma((nyc,)),
            dma((ndp + 2 * nx,)), dma((ndp + 2 * nx,)), dma((nx,)), dma((nx,)),
        ],
        compiler_params=pltpu.CompilerParams(collective_id=0, has_side_effects=True, vmem_limit_bytes=48 << 20),
        name="mlp_grads",
    )(grad_out, saved_hidden, down_weight)


def solution(mesh):
    nx, ny, nz = mesh.shape["row"] // 2, mesh.shape["dp"] * 2, mesh.shape["col"] // 2
    placed = (P(("dp", "col"), "row"), P(("dp", "row"), "col"), P("col", "row"))
    return jax.shard_map(
        functools.partial(local, nx, ny, nz),
        mesh=mesh,
        in_specs=placed,
        out_specs=(P(("dp", "row"), "col"), P(("col", "dp"), "row")),
        check_vma=False,
    )
```

time: 212 us -> 69.5 us (0.33)
  the two profiles are of different devices: /device:TPU:5 before, /device:TPU:8 now
where the time goes in v1:
time: 69.5 us; the launch traced here: 69.2 us
  Pallas kernels  64.2 us (92%)
  local copies, waits for them, and re-layouts  4.36 us (6%)
    pallas_call x1, Pallas kernels, local(): pl.pallas_call(functools.partial(kernel, nx, ny, nz), out_shape=(jax.Shap...  64.2 us
    unnamed x8, local copies, waits for them, and re-layouts  4.36 us

profile of v1, /device:TPU:8, one launch (start us, length us, event | category | flops | bytes accessed | tf_op | source)
XLA Modules:
  0.0 69.2 jit_solution(13694744816358646894)
XLA Ops:
  0.6 0.0 copy-start
  0.6 1.4 %copy-done = bf16[832,1024]{1,0:T(8,128)(2,1)S(1)} copy-done((bf16[832,1024]{1,0:T(8,128)(2,1)S(1)}, bf16[832,1024]{1,0:T(8,128)(2,1)}, u32[]{:S(2)}) %copy-start) | copy-done | bytes 1703960
  2.1 0.0 copy-start.1
  2.1 0.8 %copy-done.1 = bf16[32,832]{1,0:T(8,128)(2,1)S(1)} copy-done((bf16[32,832]{1,0:T(8,128)(2,1)S(1)}, bf16[32,832]{1,0:T(8,128)(2,1)}, u32[]{:S(2)}) %copy-start.1) | copy-done | bytes 53272
  2.9 0.0 copy-start.2
  2.9 0.7 %copy-done.2 = bf16[8,1024]{1,0:T(8,128)(2,1)S(1)} copy-done((bf16[8,1024]{1,0:T(8,128)(2,1)S(1)}, bf16[8,1024]{1,0:T(8,128)(2,1)}, u32[]{:S(2)}) %copy-start.2) | copy-done | bytes 16408
  3.6 64.2 %mlp_grads.1 = (bf16[32,832]{1,0:T(8,128)(2,1)S(1)}, bf16[208,1024]{1,0:T(8,128)(2,1)S(1)}) custom-call(bf16[8,1024]{1,0:T(8,128)(2,1)S(1)} %copy-done.2, bf16[32,832]{1,0:T(8,128)(2,1)S(1)} %copy-done.1, bf16[832,1024]{1,0:T(8,128)(2,1)S(1)} %copy-done), custom_call_target="tpu_custom_call" | custom-call | tf_op jit(solution)/shard_map/mlp_grads/pallas_call | solution.py:243
  67.8 0.6 copy.7
  68.4 0.8 %copy.8 = bf16[208,1024]{1,0:T(8,128)(2,1)} copy(bf16[208,1024]{1,0:T(8,128)(2,1)S(1)} %get-tuple-element.5) | data formatting | bytes 851968
Async XLA Ops:
  0.6 1.5 %copy-start = (bf16[832,1024]{1,0:T(8,128)(2,1)S(1)}, bf16[832,1024]{1,0:T(8,128)(2,1)}, u32[]{:S(2)}) copy-start(bf16[832,1024]{1,0:T(8,128)(2,1)} %w_hbm.1) | copy-start | bytes 5111812
  2.1 0.8 %copy-start.1 = (bf16[32,832]{1,0:T(8,128)(2,1)S(1)}, bf16[32,832]{1,0:T(8,128)(2,1)}, u32[]{:S(2)}) copy-start(bf16[32,832]{1,0:T(8,128)(2,1)} %h_hbm.1) | copy-start | bytes 159748
  2.9 0.7 %copy-start.2 = (bf16[8,1024]{1,0:T(8,128)(2,1)S(1)}, bf16[8,1024]{1,0:T(8,128)(2,1)}, u32[]{:S(2)}) copy-start(bf16[8,1024]{1,0:T(8,128)(2,1)} %g_hbm.1) | copy-start | bytes 49156

commit v2 on v0

v2 whole, which is shorter than its diff:
```python
import functools

import jax
import jax.numpy as jnp
from jax import lax
from jax.experimental import pallas as pl
from jax.experimental.pallas import tpu as pltpu
from jax.sharding import PartitionSpec as P

MESH = pl.DeviceIdType.MESH
F32, BF16 = jnp.float32, jnp.bfloat16
LAG = 3
H_AT = (0, 3, 6, 8)
SEND = {0: [(2, 3)], 1: [(0, 1), (1, 2)], 2: [(1, 3)], 3: [(0, 2), (0, 3)]}
FROM = {0: [0], 1: [1], 3: [2, 3]}
NEAR = 4
Z_FIRST = False


def rel_of(slot, n):
    return (-((slot + 1) // 2) if slot % 2 else slot // 2) % n


def kernel(nx, ny, nz, g_hbm, h_hbm, w_hbm, ig_ref, wg_ref, gb, hv, hs, hb, ht, wv, ps, pr, mine, rr, acc,
           lsem, zs, zr, ys, yr, hss, hrs, iss, irs, in_z, in_o):
    ndp = ny // 2
    hid = h_hbm.shape[1]
    quarter = hid // ndp
    tg, cols = g_hbm.shape
    th = h_hbm.shape[0]
    per = th // tg
    nq = nz // per
    size = 2 if per % 2 == 0 else 1
    ng = nz // size
    top = ny // 2
    dp, row, col = (lax.axis_index(a) for a in ("dp", "row", "col"))
    y_lo, z = lax.div(col, nz), lax.rem(col, nz)
    y = dp * 2 + y_lo
    x, c = lax.div(row, 2), lax.rem(row, 2)

    def dev(x_=None, y_=None, z_=None, c_=None):
        xx, yy = (x if x_ is None else x_), (y if y_ is None else y_)
        zz, cc = (z if z_ is None else z_), (c if c_ is None else c_)
        return (lax.div(yy, 2), xx * 2 + cc, lax.rem(yy, 2) * nz + zz)

    def signal(sem, to):
        pl.semaphore_signal(sem, inc=1, device_id=to, device_id_type=MESH)

    def wait(sem, n):
        @pl.when(n > 0)
        def _():
            pl.semaphore_wait(sem, n)

    def remote(src, dst, ss, rs, to):
        return pltpu.make_async_remote_copy(src_ref=src, dst_ref=dst, send_sem=ss, recv_sem=rs, device_id=to, device_id_type=MESH)

    def up(d):
        return lax.rem(y + d, ny)

    y_near = sorted({1, ny - 1})
    y_far = list(range(2, ny, 2))
    peers = [(dev(y_=up(d)), up(d) > y, 0) for d in y_near] + [(dev(y_=up(d)), up(d) > y, 1) for d in y_far]
    peers += [(dev(x_=lax.rem(x + d, nx)), lax.rem(x + d, nx) > x, 2) for d in range(1, nx)]
    peers += [(dev(c_=1 - c), c == 0, 3)]

    load_g = pltpu.make_async_copy(g_hbm, gb.at[0, z], lsem.at[0])
    load_h = pltpu.make_async_copy(h_hbm, hv, lsem.at[1])
    load_w = pltpu.make_async_copy(w_hbm, wv, lsem.at[2])
    load_g.start()
    load_h.start()
    load_w.start()
    barrier = pltpu.get_barrier_semaphore()
    run, place = lax.div(z, NEAR), lax.rem(z, NEAR)
    before = jnp.int32(0)
    is_near = [jnp.logical_and(run == k // NEAR, k != z) for k in range(nz)]
    is_far = [jnp.logical_and(place == k % NEAR, k != z) for k in range(nz)]
    is_peer = [jnp.logical_or(n, f) for n, f in zip(is_near, is_far)]
    for k in range(nz):
        pl.when(jnp.logical_and(is_peer[k], k > z))(functools.partial(signal, barrier, dev(z_=k)))
        before = before + jnp.where(jnp.logical_and(is_peer[k], k < z), 1, 0)
    later = [0, 0, 0, 0]
    for to, is_later, kind in peers:
        pl.when(is_later)(functools.partial(signal, barrier, to))
        n = jnp.where(is_later, 1, 0)
        before = before + 1 - n
        later[kind] = later[kind] + n
    load_h.wait()
    hs[...] = jnp.zeros_like(hs)
    for k in range(ndp):
        hs[k, :, :quarter] = hv[:, k * quarter:(k + 1) * quarter]
    hb[row, dp] = hs[dp]
    load_g.wait()
    wait(barrier, before)

    def z_copy(k, to, sem):
        return remote(gb.at[0, k], gb.at[0, k], zs.at[sem], zr.at[k], dev(z_=to))

    def near_sem(to, k):
        return lax.rem(to, NEAR) * (nz // NEAR) + lax.div(k, NEAR)

    def far_sem(to):
        return nz + to // NEAR

    def to_earlier(k):
        signal(in_z.at[z], dev(z_=k))

        @pl.when(is_near[k])
        def _():
            z_copy(z, k, near_sem(k, z)).start()

        @pl.when(is_far[k])
        def _():
            z_copy(z, k, far_sem(k)).start()

    for k in range(nz):
        pl.when(jnp.logical_and(is_peer[k], k < z))(functools.partial(to_earlier, k))
    for to, is_later, kind in peers:
        pl.when(jnp.logical_not(is_later))(functools.partial(signal, in_o.at[kind], to))

    def y_copy(up_, level, g):
        s0, n = g * size, size
        if level == top:
            if n == 1:
                if (g % 2 == 0) != up_:
                    return None
            else:
                s0, n = s0 + (0 if up_ else 1), 1
        frm = 0 if level == 1 else (2 * level - 3 if up_ else 2 * level - 2)
        to = ny - 1 if level == top else (2 * level - 1 if up_ else 2 * level)
        k = ((level - 1) * 2 + (0 if up_ else 1)) * ng + g
        return remote(gb.at[frm, pl.ds(s0, n)], gb.at[to, pl.ds(s0, n)], ys.at[k], yr.at[k], dev(y_=up(1 if up_ else ny - 1)))

    yc = {(u, l, g): y_copy(u, l, g) for u in (True, False) for l in range(1, top + 1) for g in range(ng)}
    sent = []

    def send(cp):
        if cp is not None:
            cp.start()
            sent.append(cp)

    def y_send(level, g):
        for u in (True, False):
            send(yc[u, level, g])

    h1 = []
    for j, d in enumerate(y_far):
        to_dp = lax.rem(dp + d // 2, ndp)
        h1.append(remote(hs.at[to_dp], hb.at[row, dp], hss.at[j], hrs.at[j], dev(y_=up(d))))
    h2 = [remote(hb.at[row], hb.at[row], hss.at[ndp + j], hrs.at[ndp + j], dev(x_=lax.rem(x + d, nx)))
          for j, d in enumerate(range(1, nx))]
    h3 = []
    for j in range(nx):
        r = lax.rem(x + nx - j, nx) * 2 + c
        k = ndp + nx + j
        h3.append(remote(hb.at[r], hb.at[r], hss.at[k], hrs.at[k], dev(c_=1 - c)))

    def do_h1():
        wait(in_o.at[1], later[1])
        for cp in h1:
            send(cp)

    def do_h2():
        for cp in h1:
            cp.wait_recv()
        wait(in_o.at[2], later[2])
        for cp in h2:
            send(cp)
        wait(in_o.at[3], later[3])
        send(h3[0])

    def do_h3():
        for j, cp in enumerate(h2):
            cp.wait_recv()
            send(h3[j + 1])

    def do_ht():
        for cp in h3:
            cp.wait_recv()
        for q in range(nq):
            parts = []
            for o in range(ny):
                yy = up(rel_of(o, ny))
                parts.append(hb[lax.rem(yy, 2) * nq + q, lax.div(yy, 2)])
            ht[q] = jnp.concatenate(parts, 0).T

    def partial(q):
        own = gb[0, per * q:per * (q + 1)].reshape(th, cols)
        other = gb[jnp.where(y_lo == 0, 2, 1) if top > 1 else 1, per * q:per * (q + 1)].reshape(th, cols)
        xg = jnp.concatenate([own, other], 0)
        p = lax.dot_general(xg, wv[...], (((1,), (1,)), ((), ())), preferred_element_type=F32)
        ps[q, y_lo] = p[:th]
        ps[q, 1 - y_lo] = p[th:]

    r1 = [remote(ps.at[q], pr.at[q // 2], iss.at[q], irs.at[q], dev(c_=1 - c)) for q in range(nq)]

    def r2_of(q, half):
        to_x = half * (nx // 2) + q // 2
        j = lax.rem(x - to_x + nx, nx) - 1
        return to_x, remote(pr.at[q // 2, half], rr.at[j], iss.at[nq + (q // 2) * 2 + half], irs.at[nq + j], dev(x_=to_x))

    def do_partial(q):
        partial(q)
        pl.when(c != q % 2)(r1[q].start)

    def do_sum(q):
        @pl.when(c == q % 2)
        def _():
            r1[q].wait_recv()
            for half in range(2):
                to_x, cp = r2_of(q, half)
                pr[q // 2, half] = pr[q // 2, half] + ps[q, half]

                @pl.when(x != to_x)
                def _():
                    cp.start()

                @pl.when(x == to_x)
                def _():
                    mine[...] = pr[q // 2, half]

    def do_total():
        total = mine[...]
        for j in range(nx - 1):
            remote(rr.at[j], rr.at[j], iss.at[j], irs.at[nq + j], dev(c_=1 - c)).wait_recv()
            total = total + rr[j]
        ig_ref[...] = total.astype(BF16)

    def do_weight(q):
        blk = gb[:, per * q:per * (q + 1)].reshape(ny * th, cols)
        t = jnp.dot(ht[q], blk, preferred_element_type=F32)[:quarter]
        if q:
            t = acc[...] + t
        if q < nq - 1:
            acc[...] = t
        else:
            wg_ref[...] = t.astype(BF16)

    def to_later_near(p):
        @pl.when(jnp.logical_and(is_near[p], p > z))
        def _():
            pl.semaphore_wait(in_z.at[p], 1)
            z_copy(z, p, near_sem(p, z)).start()

    def to_later_run(of, to):
        @pl.when(run == of)
        def _():
            p = to * NEAR + place
            pl.semaphore_wait(in_z.at[p], 1)
            z_copy(z, p, nz + to).start()

    def from_run(r):
        @pl.when(run != r)
        def _():
            k = r * NEAR + place
            z_copy(k, z, 0).wait_recv()
            for m in range(NEAR):
                p = run * NEAR + m

                @pl.when(m != place)
                def _():
                    z_copy(k, p, near_sem(p, k)).start()

    def z_step(g):
        if g == 0:
            for p in range(nz):
                to_later_near(p)
        for of, to in SEND.get(g, ()):
            to_later_run(of, to)
        for r in FROM.get(g, ()):
            from_run(r)
        for k in range(g * size, (g + 1) * size):
            @pl.when(jnp.logical_and(k != z, jnp.logical_not(is_far[k])))
            def _():
                z_copy(k, z, 0).wait_recv()
        if g == 0:
            wait(in_o.at[0], later[0])
        y_send(1, g)

    def y_step(level, g):
        for u in (True, False):
            if yc[u, level, g] is not None:
                yc[u, level, g].wait_recv()
        if level < top:
            y_send(level + 1, g)

    gq = per // size
    todo = {}

    def plan(r, f, *a):
        todo.setdefault(r, []).append(functools.partial(f, *a))

    for r, f in zip(H_AT, (do_h1, do_h2, do_h3, do_ht)):
        plan(r, f)
    plan(0, load_w.wait)
    for q in range(nq):
        last = (q + 1) * gq - 1
        plan(last + LAG, do_partial, q)
        plan(last + LAG + 1, do_sum, q)
        plan(last + LAG * top + (q < nq - 1), do_weight, q)
    plan(ng + LAG * top, do_total)
    for r in range(ng + LAG * top + 1):
        def zz():
            if r < ng:
                z_step(r)
        if Z_FIRST:
            zz()
        for level in range(1, top + 1):
            g = r - LAG * level
            if 0 <= g < ng:
                y_step(level, g)
        if not Z_FIRST:
            zz()
        for f in todo.pop(r, []):
            f()
    assert not todo
    for cp in sent:
        cp.wait_send()
    for p in range(nz):
        @pl.when(is_near[p])
        def _():
            for r in range(nz // NEAR):
                k = r * NEAR + place
                z_copy(k, p, near_sem(p, k)).wait_send()

        @pl.when(is_far[p])
        def _():
            z_copy(z, p, far_sem(p)).wait_send()
    for q in range(nq):
        pl.when(c != q % 2)(r1[q].wait_send)
        for half in range(2):
            to_x, cp = r2_of(q, half)
            pl.when(jnp.logical_and(c == q % 2, x != to_x))(cp.wait_send)


def local(nx, ny, nz, grad_out, saved_hidden, down_weight):
    tg, cols = grad_out.shape
    th, hid = saved_hidden.shape
    ndp = ny // 2
    quarter = hid // ndp
    wide = -(-quarter // 128) * 128
    nq = nz // (th // tg)
    nyc = 2 * (ny // 2) * nz
    dma, reg = pltpu.SemaphoreType.DMA, pltpu.SemaphoreType.REGULAR
    return pl.pallas_call(
        functools.partial(kernel, nx, ny, nz),
        out_shape=(jax.ShapeDtypeStruct((th, hid), BF16), jax.ShapeDtypeStruct((quarter, cols), BF16)),
        in_specs=[pl.BlockSpec(memory_space=pltpu.HBM)] * 3,
        out_specs=(pl.BlockSpec(memory_space=pltpu.VMEM),) * 2,
        scratch_shapes=[
            pltpu.VMEM((ny, nz, tg, cols), BF16),
            pltpu.VMEM((th, hid), BF16),
            pltpu.VMEM((ndp, th, wide), BF16),
            pltpu.VMEM((2 * nx, ndp, th, wide), BF16),
            pltpu.VMEM((nq, wide, ny * th), BF16),
            pltpu.VMEM(down_weight.shape, BF16),
            pltpu.VMEM((nq, 2, th, hid), F32),
            pltpu.VMEM((nq // 2, 2, th, hid), F32),
            pltpu.VMEM((th, hid), F32),
            pltpu.VMEM((nx - 1, th, hid), F32),
            pltpu.VMEM((quarter, cols), F32),
            dma((3,)), dma((nz + nz // NEAR,)), dma((nz,)), dma((nyc,)), dma((nyc,)),
            dma((ndp + 2 * nx,)), dma((ndp + 2 * nx,)), dma((2 * nq,)), dma((2 * nq,)),
            reg((nz,)), reg((4,)),
        ],
        compiler_params=pltpu.CompilerParams(collective_id=0, has_side_effects=True, vmem_limit_bytes=53 << 20),
        name="mlp_grads",
    )(grad_out, saved_hidden, down_weight)


def solution(mesh):
    nx, ny, nz = mesh.shape["row"] // 2, mesh.shape["dp"] * 2, mesh.shape["col"] // 2
    placed = (P(("dp", "col"), "row"), P(("dp", "row"), "col"), P("col", "row"))
    return jax.shard_map(
        functools.partial(local, nx, ny, nz),
        mesh=mesh,
        in_specs=placed,
        out_specs=(P(("dp", "row"), "col"), P(("col", "dp"), "row")),
        check_vma=False,
    )
```

time: 212 us -> 58.4 us (0.28)
  the two profiles are of different devices: /device:TPU:5 before, /device:TPU:704 now
where the time goes in v2:
time: 58.4 us; the launch traced here: 58.1 us
  Pallas kernels  54.6 us (93%)
  local copies, waits for them, and re-layouts  2.91 us (5%)
  between operations  0.65 us (1%)
    pallas_call x1, Pallas kernels, local(): pl.pallas_call(functools.partial(kernel, nx, ny, nz), out_shape=(jax.Shap...  54.6 us
    unnamed x6, local copies, waits for them, and re-layouts  2.91 us

profile of v2, /device:TPU:704, one launch (start us, length us, event | category | flops | bytes accessed | tf_op | source)
XLA Modules:
  0.0 58.1 jit_solution(15522571265191566869)
XLA Ops:
  0.6 0.0 copy-start
  0.6 0.8 %copy-done = bf16[32,832]{1,0:T(8,128)(2,1)S(1)} copy-done((bf16[32,832]{1,0:T(8,128)(2,1)S(1)}, bf16[32,832]{1,0:T(8,128)(2,1)}, u32[]{:S(2)}) %copy-start) | copy-done | bytes 53272
  1.4 0.0 copy-start.1
  1.5 0.7 %copy-done.1 = bf16[8,1024]{1,0:T(8,128)(2,1)S(1)} copy-done((bf16[8,1024]{1,0:T(8,128)(2,1)S(1)}, bf16[8,1024]{1,0:T(8,128)(2,1)}, u32[]{:S(2)}) %copy-start.1) | copy-done | bytes 16408
  2.2 54.6 %mlp_grads.1 = (bf16[32,832]{1,0:T(8,128)(2,1)S(1)}, bf16[208,1024]{1,0:T(8,128)(2,1)S(1)}) custom-call(bf16[8,1024]{1,0:T(8,128)(2,1)S(1)} %copy-done.1, bf16[32,832]{1,0:T(8,128)(2,1)S(1)} %copy-done, bf16[832,1024]{1,0:T(8,128)(2,1)} %w_hbm.1), custom_call_target="tpu_custom_call" | custom-call | tf_op jit(solution)/shard_map/mlp_grads/pallas_call | solution.py:344
  56.7 0.6 %copy.7 = bf16[32,832]{1,0:T(8,128)(2,1)} copy(bf16[32,832]{1,0:T(8,128)(2,1)S(1)} %get-tuple-element.4) | data formatting | bytes 106496
  57.4 0.8 %copy.8 = bf16[208,1024]{1,0:T(8,128)(2,1)} copy(bf16[208,1024]{1,0:T(8,128)(2,1)S(1)} %get-tuple-element.5) | data formatting | bytes 851968
Async XLA Ops:
  0.6 0.8 %copy-start = (bf16[32,832]{1,0:T(8,128)(2,1)S(1)}, bf16[32,832]{1,0:T(8,128)(2,1)}, u32[]{:S(2)}) copy-start(bf16[32,832]{1,0:T(8,128)(2,1)} %h_hbm.1) | copy-start | bytes 159748
  1.4 0.7 %copy-start.1 = (bf16[8,1024]{1,0:T(8,128)(2,1)S(1)}, bf16[8,1024]{1,0:T(8,128)(2,1)}, u32[]{:S(2)}) copy-start(bf16[8,1024]{1,0:T(8,128)(2,1)} %g_hbm.1) | copy-start | bytes 49156

commit v3 on v2

--- a/solution.py
+++ b/solution.py
@@ -9,10 +9,10 @@
 
 MESH = pl.DeviceIdType.MESH
 F32, BF16 = jnp.float32, jnp.bfloat16
-LAG = 3
-H_AT = (0, 3, 6, 8)
-SEND = {0: [(2, 3)], 1: [(0, 1), (1, 2)], 2: [(1, 3)], 3: [(0, 2), (0, 3)]}
-FROM = {0: [0], 1: [1], 3: [2, 3]}
+LAG = 4
+H_AT = (0, 3, 6, 9)
+SEND = {0: [(2, 3)], 1: [(0, 1), (1, 2)], 2: [(1, 3), (0, 2), (0, 3)]}
+FROM = {0: [0], 1: [1], 2: [2], 3: [3]}
 NEAR = 4
 Z_FIRST = False
 

time: 58.4 us -> 56.9 us (0.974)
  Pallas kernels: 54.6 us -> 53.1 us
    pallas_call x1, Pallas kernels: 54.6 us -> 53.1 us  [local(): pl.pallas_call(functools.partial(kernel, nx, ny, nz), out_shape=(jax.Shap...]
where the time goes in v3:
time: 56.9 us; the launch traced here: 56.6 us
  Pallas kernels  53.1 us (93%)
  local copies, waits for them, and re-layouts  2.91 us (5%)
  between operations  0.65 us (1%)
    pallas_call x1, Pallas kernels, local(): pl.pallas_call(functools.partial(kernel, nx, ny, nz), out_shape=(jax.Shap...  53.1 us
    unnamed x6, local copies, waits for them, and re-layouts  2.91 us

profile of v3, /device:TPU:704, one launch (start us, length us, event | category | flops | bytes accessed | tf_op | source)
XLA Modules:
  0.0 56.6 jit_solution(17296223377239521603)
XLA Ops:
  0.6 0.0 copy-start
  0.6 0.8 %copy-done = bf16[32,832]{1,0:T(8,128)(2,1)S(1)} copy-done((bf16[32,832]{1,0:T(8,128)(2,1)S(1)}, bf16[32,832]{1,0:T(8,128)(2,1)}, u32[]{:S(2)}) %copy-start) | copy-done | bytes 53272
  1.4 0.0 copy-start.1
  1.5 0.7 %copy-done.1 = bf16[8,1024]{1,0:T(8,128)(2,1)S(1)} copy-done((bf16[8,1024]{1,0:T(8,128)(2,1)S(1)}, bf16[8,1024]{1,0:T(8,128)(2,1)}, u32[]{:S(2)}) %copy-start.1) | copy-done | bytes 16408
  2.2 53.1 %mlp_grads.1 = (bf16[32,832]{1,0:T(8,128)(2,1)S(1)}, bf16[208,1024]{1,0:T(8,128)(2,1)S(1)}) custom-call(bf16[8,1024]{1,0:T(8,128)(2,1)S(1)} %copy-done.1, bf16[32,832]{1,0:T(8,128)(2,1)S(1)} %copy-done, bf16[832,1024]{1,0:T(8,128)(2,1)} %w_hbm.1), custom_call_target="tpu_custom_call" | custom-call | tf_op jit(solution)/shard_map/mlp_grads/pallas_call | solution.py:344
  55.2 0.6 %copy.7 = bf16[32,832]{1,0:T(8,128)(2,1)} copy(bf16[32,832]{1,0:T(8,128)(2,1)S(1)} %get-tuple-element.4) | data formatting | bytes 106496
  55.9 0.8 %copy.8 = bf16[208,1024]{1,0:T(8,128)(2,1)} copy(bf16[208,1024]{1,0:T(8,128)(2,1)S(1)} %get-tuple-element.5) | data formatting | bytes 851968
Async XLA Ops:
  0.6 0.8 %copy-start = (bf16[32,832]{1,0:T(8,128)(2,1)S(1)}, bf16[32,832]{1,0:T(8,128)(2,1)}, u32[]{:S(2)}) copy-start(bf16[32,832]{1,0:T(8,128)(2,1)} %h_hbm.1) | copy-start | bytes 159748
  1.4 0.7 %copy-start.1 = (bf16[8,1024]{1,0:T(8,128)(2,1)S(1)}, bf16[8,1024]{1,0:T(8,128)(2,1)}, u32[]{:S(2)}) copy-start(bf16[8,1024]{1,0:T(8,128)(2,1)} %g_hbm.1) | copy-start | bytes 49156

commit v4 on v3

--- a/solution.py
+++ b/solution.py
@@ -343,7 +343,7 @@
     dma, reg = pltpu.SemaphoreType.DMA, pltpu.SemaphoreType.REGULAR
     return pl.pallas_call(
         functools.partial(kernel, nx, ny, nz),
-        out_shape=(jax.ShapeDtypeStruct((th, hid), BF16), jax.ShapeDtypeStruct((quarter, cols), BF16)),
+        out_shape=(pltpu.VMEM((th, hid), BF16), pltpu.VMEM((quarter, cols), BF16)),
         in_specs=[pl.BlockSpec(memory_space=pltpu.HBM)] * 3,
         out_specs=(pl.BlockSpec(memory_space=pltpu.VMEM),) * 2,
         scratch_shapes=[
@@ -362,7 +362,7 @@
             dma((ndp + 2 * nx,)), dma((ndp + 2 * nx,)), dma((2 * nq,)), dma((2 * nq,)),
             reg((nz,)), reg((4,)),
         ],
-        compiler_params=pltpu.CompilerParams(collective_id=0, has_side_effects=True, vmem_limit_bytes=53 << 20),
+        compiler_params=pltpu.CompilerParams(collective_id=0, has_side_effects=True, vmem_limit_bytes=54 << 20),
         name="mlp_grads",
     )(grad_out, saved_hidden, down_weight)
 

time: 56.9 us -> 55.1 us (0.968)
  local copies, waits for them, and re-layouts: 2.91 us -> 1.38 us
    unnamed x6 -> x2, local copies, waits for them, and re-layouts: 2.91 us -> 1.38 us
where the time goes in v4:
time: 55.1 us; the launch traced here: 55 us
  Pallas kernels  53 us (96%)
  local copies, waits for them, and re-layouts  1.38 us (3%)
  between operations  0.64 us (1%)
    pallas_call x1, Pallas kernels, local(): pl.pallas_call(functools.partial(kernel, nx, ny, nz), out_shape=(pltpu.VM...  53 us
    unnamed x2, local copies, waits for them, and re-layouts  1.38 us

profile of v4, /device:TPU:704, one launch (start us, length us, event | category | flops | bytes accessed | tf_op | source)
XLA Modules:
  0.0 55.0 jit_solution(14800886488697208304)
XLA Ops:
  0.6 53.0 %mlp_grads.1 = (bf16[32,832]{1,0:T(8,128)(2,1)S(1)}, bf16[208,1024]{1,0:T(8,128)(2,1)S(1)}) custom-call(bf16[8,1024]{1,0:T(8,128)(2,1)} %g_hbm.1, bf16[32,832]{1,0:T(8,128)(2,1)} %h_hbm.1, bf16[832,1024]{1,0:T(8,128)(2,1)} %w_hbm.1), custom_call_target="tpu_custom_call" | custom-call | tf_op jit(solution)/shard_map/mlp_grads/pallas_call | solution.py:344
  53.6 0.6 %copy.7 = bf16[32,832]{1,0:T(8,128)(2,1)} copy(bf16[32,832]{1,0:T(8,128)(2,1)S(1)} %get-tuple-element.2) | data formatting | bytes 106496
  54.2 0.8 %copy.8 = bf16[208,1024]{1,0:T(8,128)(2,1)} copy(bf16[208,1024]{1,0:T(8,128)(2,1)S(1)} %get-tuple-element.3) | data formatting | bytes 851968
